TPU v7x, 32 devices: a whole 2x2x4 slice. The times are simulated.
32 devices in a mesh: dp: 16 (over z, y, x), tile: 2 (over core).
Axes of the slice: x: 2, y: 2, z: 4, core: 2. Of those that a mesh axis runs over, the one named last changes fastest.
Arguments:
- feats: bfloat16 [1024, 2048], P('dp'), may hold values from -11 to 11
- jitter: bfloat16 [1024, 2048], P('dp'), may hold values from -1.5 to 1.5
- mask_ids: int32 [1024, 2], P('dp'), may hold values from 0 to 31
- proj_weight: bfloat16 [2048, 4096], P('dp', 'tile'), may hold values from -0.125 to 0.125
Outputs:
- feats_grad: float32 [1024, 2048], P('dp', 'tile')
- diag_corr: float32 [4096], P('tile')
- cross_power: float32 [], replicated
All inputs are finite; a program needn't handle non-finite values.
Results may differ from a plain program's by a relative error of at most 0.02.
Values may be sent and summed in bfloat16 or wider, within the bound.
A program may use at most 64 MiB of HBM per device.

v0:
```python
import jax
import jax.numpy as jnp
from jax import lax
from jax.sharding import PartitionSpec as P

EMB = 4096
GROUPS = 32


LAMBDA_OFF = 0.0051
NORM_EPS = 1e-05
LOSS_SCALE = 65536.0


def masked_views(feats, jitter, mask_ids):
    width = feats.shape[1]
    group_size = width // GROUPS
    channel_group = lax.broadcasted_iota(jnp.int32, (1, width), 1) // group_size
    keep_a = (channel_group != mask_ids[:, 0:1]).astype(jnp.float32)
    keep_b = (channel_group != mask_ids[:, 1:2]).astype(jnp.float32)
    values = feats.astype(jnp.float32)
    view_a = (values * keep_a).astype(jnp.bfloat16)
    view_b = (values * keep_b + jitter.astype(jnp.float32)).astype(jnp.bfloat16)
    return (view_a, view_b, keep_a, keep_b)


def contract_last(left, right):
    return lax.dot_general(
        left, right, (((1,), (1,)), ((), ())), preferred_element_type=jnp.float32
    )


def on_device(feats, jitter, mask_ids, proj_weight):
    view_a, view_b, keep_a, keep_b = masked_views(feats, jitter, mask_ids)
    rows = feats.shape[0]
    total = rows * lax.axis_size("dp")
    piece = lax.all_gather(proj_weight, "dp", axis=0, tiled=True)
    raw_a = jnp.dot(view_a, piece, preferred_element_type=jnp.float32)
    raw_b = jnp.dot(view_b, piece, preferred_element_type=jnp.float32)
    raw_a = raw_a.astype(jnp.bfloat16)
    raw_b = raw_b.astype(jnp.bfloat16)
    values_a = raw_a.astype(jnp.float32)
    values_b = raw_b.astype(jnp.float32)
    moment_sums = lax.psum(
        (
            jnp.sum(values_a, axis=0),
            jnp.sum(values_a * values_a, axis=0),
            jnp.sum(values_b, axis=0),
            jnp.sum(values_b * values_b, axis=0),
        ),
        "dp",
    )
    mean_a = moment_sums[0] / total
    mean_b = moment_sums[2] / total
    inv_a = lax.rsqrt(moment_sums[1] / total - mean_a * mean_a + NORM_EPS)
    inv_b = lax.rsqrt(moment_sums[3] / total - mean_b * mean_b + NORM_EPS)
    norm_a = ((values_a - mean_a) * inv_a).astype(jnp.bfloat16)
    norm_b = ((values_b - mean_b) * inv_b).astype(jnp.bfloat16)
    outgoing_a, outgoing_b = (norm_a, norm_b)
    gathered_a, gathered_b = (
        lax.all_gather(outgoing_a, "dp", axis=0, tiled=True),
        lax.all_gather(outgoing_b, "dp", axis=0, tiled=True),
    )
    whole_a, whole_b = (gathered_a, gathered_b)
    za = norm_a.astype(jnp.float32)
    zb = norm_b.astype(jnp.float32)
    diag_corr = jnp.sum(whole_a.astype(jnp.float32) * whole_b.astype(jnp.float32), axis=0) / total
    gram_a, gram_b = (
        lax.psum(contract_last(norm_a, whole_a).astype(jnp.bfloat16), "tile").astype(jnp.float32),
        lax.psum(contract_last(norm_b, whole_b).astype(jnp.bfloat16), "tile").astype(jnp.float32),
    )
    trace_part = jnp.sum(gram_a * gram_b)
    gram_bf_a = gram_a.astype(jnp.bfloat16)
    gram_bf_b = gram_b.astype(jnp.bfloat16)
    coeff = -2.0 * (1.0 - diag_corr) - 2.0 * LAMBDA_OFF * diag_corr
    factor = 2.0 * LAMBDA_OFF / (total * total)
    grad_na = zb * coeff / total + factor * jnp.dot(
        gram_bf_b, whole_a, preferred_element_type=jnp.float32
    )
    grad_nb = za * coeff / total + factor * jnp.dot(
        gram_bf_a, whole_b, preferred_element_type=jnp.float32
    )
    sums = lax.psum(
        (
            jnp.sum(grad_na, axis=0),
            jnp.sum(grad_na * za, axis=0),
            jnp.sum(grad_nb, axis=0),
            jnp.sum(grad_nb * zb, axis=0),
            trace_part,
        ),
        "dp",
    )
    dz_a = (inv_a * (grad_na - sums[0] / total - za * (sums[1] / total))).astype(jnp.bfloat16)
    dz_b = (inv_b * (grad_nb - sums[2] / total - zb * (sums[3] / total))).astype(jnp.bfloat16)
    cross_power = sums[4] / (total * total) / EMB
    piece = lax.all_gather(proj_weight, "dp", axis=0, tiled=True)
    combined = keep_a * contract_last(dz_a, piece) + keep_b * contract_last(dz_b, piece)
    feats_grad = LOSS_SCALE * lax.psum_scatter(
        combined.astype(jnp.bfloat16), "tile", scatter_dimension=1, tiled=True
    ).astype(jnp.float32)
    return (feats_grad, diag_corr, cross_power)


def solution(mesh):
    in_specs = (P("dp", None), P("dp", None), P("dp", None), P("dp", "tile"))
    out_specs = (P("dp", "tile"), P("tile"), P())
    return jax.shard_map(
        on_device, mesh=mesh, in_specs=in_specs, out_specs=out_specs, check_vma=False
    )
```

profile of v0, /device:TPU:0, one launch (start us, length us, event | category | flops | bytes accessed | tf_op | source)
XLA Modules:
  0.0 492.4 jit_solution(9613232110448634272)
XLA Ops:
  7.2 0.7 all-gather.4.cloned.1.call-update
  8.0 0.8 slice_bitcast_fusion
  8.7 117.6 %all-gather.4.cloned.1.call-done = bf16[2048,2048]{1,0:T(8,128)(2,1)} async-done(((bf16[128,2048]{1,0:T(8,128)(2,1)}), bf16[2048,2048]{1,0:T(8,128)(2,1)}) %all-gather.4.cloned.1.call-update) | async-done | bytes 8388624 | tf_op jit(solution)/shard_map/all_gather | solution.py:37
  126.3 5.3 %multiply_reduce_fusion.2 = (f32[2048]{0:T(1024)S(1)}, f32[2048]{0:T(1024)S(1)}, f32[64,2048]{1,0:T(8,128)S(1)}) fusion(bf16[2048,2048]{1,0:T(8,128)(2,1)} %all-gather.4.cloned.1.call-done, bf16[64,2048]{1,0:T(8,128)(2,1)} %param.4, s32[2048]{0:T(1024)S(1)} %add_select_fusion, s32[64]{0:T(128)S(1)} %get-tuple-element.29), kind=kOutput, calls=%fused_computation.39 | convolution fusion | flops 538046464 | bytes 9199872 | tf_op jit(solution)/shard_map/dot_general | solution.py:38
  131.6 0.6 copy-done
  132.2 1.7 fusion.42
  133.9 74.0 %all-reduce.1 = (f32[2048]{0:T(1024)S(1)}, f32[2048]{0:T(1024)S(1)}, f32[2048]{0:T(1024)S(1)}, f32[2048]{0:T(1024)S(1)}) all-reduce(f32[2048]{0:T(1024)S(1)} %get-tuple-element.10, f32[2048]{0:T(1024)S(1)} %get-tuple-element.9, f32[2048]{0:T(1024)S(1)} %get-tuple-element.8, ...), channel_id=1, replica_groups=mesh['dp'=16,'tile'=2] {'dp'}, use_global_device_ids=true, to_apply=%region_3.4 | all-reduce | flops 8192 | bytes 65536 | tf_op jit(solution)/shard_map/psum | solution.py:44
  207.9 0.8 multiply_convert_fusion.1
  208.7 0.8 multiply_convert_fusion
  209.6 71.2 %all-gather.8.cloned.1.call-done = bf16[1024,2048]{1,0:T(8,128)(2,1)} async-done(((bf16[64,2048]{1,0:T(8,128)(2,1)}), bf16[1024,2048]{1,0:T(8,128)(2,1)}) %all-gather.8.cloned.1.call-update) | async-done | bytes 4194320 | tf_op jit(solution)/shard_map/all_gather | solution.py:62
  280.8 4.3 convolution_convert_fusion.3
  285.1 73.7 %all-gather.6.cloned.1.call-done = bf16[1024,2048]{1,0:T(8,128)(2,1)} async-done(((bf16[64,2048]{1,0:T(8,128)(2,1)}), bf16[1024,2048]{1,0:T(8,128)(2,1)}) %all-gather.6.cloned.1.call-update) | async-done | bytes 4194320 | tf_op jit(solution)/shard_map/all_gather | solution.py:61
  358.9 4.3 convolution_convert_fusion.2
  363.2 5.2 %multiply_reduce_fusion = f32[2048]{0:T(1024)S(1)} fusion(bf16[1024,2048]{1,0:T(8,128)(2,1)} %all-gather.8.cloned.1.call-done, bf16[1024,2048]{1,0:T(8,128)(2,1)} %all-gather.6.cloned.1.call-done), kind=kLoop, calls=%fused_computation | loop fusion | flops 8386560 | bytes 8396800 | tf_op jit(solution)/shard_map/reduce_sum | solution.py:67
  368.5 0.6 multiply_subtract_fusion
  369.1 11.2 %all-reduce.5.cloned.1.call-done = (bf16[64,1024]{1,0:T(8,128)(2,1)}, bf16[64,1024]{1,0:T(8,128)(2,1)}) async-done(((bf16[64,1024]{1,0:T(8,128)(2,1)}, bf16[64,1024]{1,0:T(8,128)(2,1)}), (bf16[64,1024]{1,0:T(8,128)(2,1)}, bf16[64,1024]{1,0:T(8,128)(2,1)})) %all-reduce.5.cloned.1.call-update) | async-done | bytes 262160 | tf_op jit(solution)/shard_map/psum | solution.py:70
  380.3 1.6 multiply_reduce_fusion.3
  381.9 3.3 fusion.40
  385.2 3.3 fusion.41
  388.4 78.2 %all-reduce = (f32[2048]{0:T(1024)S(1)}, f32[2048]{0:T(1024)S(1)}, f32[2048]{0:T(1024)S(1)}, f32[2048]{0:T(1024)S(1)}, f32[]{:T(128)}) all-reduce(f32[2048]{0:T(1024)S(1)} %get-tuple-element.6, f32[2048]{0:T(1024)S(1)} %get-tuple-element.5, f32[2048]{0:T(1024)S(1)} %get-tuple-element.4, ...), channel_id=1, replica_groups=mesh['dp'=16,'tile'=2] {'dp'}, use_global_device_ids=true, to_apply=%region_13.14 | all-reduce | flops 8193 | bytes 65544 | tf_op jit(solution)/shard_map/psum | solution.py:83
  466.6 6.0 %convolution_select_fusion.1 = f32[64,2048]{1,0:T(8,128)S(1)} fusion(bf16[2048,2048]{1,0:T(8,128)(2,1)} %all-gather.4.cloned.1.call-done, bf16[64,2048]{1,0:T(8,128)(2,1)S(1)} %copy-done.2, f32[64,2048]{1,0:T(8,128)S(1)} %get-tuple-element.32, f32[2048]{0:T(1024)S(1)} %get-tuple-element.36, f32[2048]{0:T(1024)S(1)} %get-tuple-element.37, ...), kind=kOutput, calls=%fused_computation.5 | convolution fusion | flops 537919488 | bytes 9732352 | tf_op jit(solution)/shard_map/dot_general | solution.py:28
  472.7 6.8 %fusion.3 = bf16[64,2048]{1,0:T(8,128)(2,1)} fusion(f32[64,2048]{1,0:T(8,128)S(1)} %convolution_select_fusion.1, bf16[2048,2048]{1,0:T(8,128)(2,1)} %all-gather.4.cloned.1.call-done, bf16[64,2048]{1,0:T(8,128)(2,1)S(1)} %copy-done.1, f32[64,2048]{1,0:T(8,128)S(1)} %get-tuple-element.33, f32[2048]{0:T(1024)S(1)} %get-tuple-element.34, ...), kind=kOutput, calls=%fused_computation.8 | convolution fusion | flops 538181632 | bytes 9994496 | tf_op jit(solution)/shard_map/dot_general | solution.py:28
  480.1 3.0 reduce-scatter.2.cloned.1.call-done
  483.1 1.6 convert_multiply_fusion.6
  (23 shorter events, 0.3 us)
Async XLA Ops:
  7.2 119.2 %all-gather.4.cloned.1.call-start = ((), (), s32[]{:S(2)}) async-start(), calls=%async_computation.1 | async-start | bytes 8912896 | tf_op jit(solution)/shard_map/all_gather | solution.py:37
  7.9 272.9 %all-gather.8.cloned.1.call-start = ((), (), s32[]{:S(2)}) async-start(), calls=%async_computation.3 | async-start | bytes 4456448 | tf_op jit(solution)/shard_map/all_gather | solution.py:62
  126.3 5.8 %copy-start = (bf16[2048,2048]{1,0:T(8,128)(2,1)S(1)}, bf16[2048,2048]{1,0:T(8,128)(2,1)}, u32[]{:S(2)}) copy-start(bf16[2048,2048]{1,0:T(8,128)(2,1)} %all-gather.4.cloned.1.call-done) | copy-start | bytes 25165828
  126.3 5.8 %copy-start.3 = (bf16[64,2048]{1,0:T(8,128)(2,1)S(1)}, bf16[64,2048]{1,0:T(8,128)(2,1)}, u32[]{:S(2)}) copy-start(bf16[64,2048]{1,0:T(8,128)(2,1)} %param.4) | copy-start | bytes 786436
  126.3 5.9 %copy-start.4 = (bf16[64,2048]{1,0:T(8,128)(2,1)S(1)}, bf16[64,2048]{1,0:T(8,128)(2,1)}, u32[]{:S(2)}) copy-start(bf16[64,2048]{1,0:T(8,128)(2,1)} %param.5) | copy-start | bytes 786436
  208.7 150.2 %all-gather.6.cloned.1.call-start = ((), (), s32[]{:S(2)}) async-start(), calls=%async_computation.2 | async-start | bytes 4456448 | tf_op jit(solution)/shard_map/all_gather | solution.py:61
  209.5 172.4 %copy-start.1 = (bf16[64,2048]{1,0:T(8,128)(2,1)S(1)}, bf16[64,2048]{1,0:T(8,128)(2,1)}, u32[]{:S(2)}) copy-start(bf16[64,2048]{1,0:T(8,128)(2,1)} %multiply_convert_fusion.1) | copy-start | bytes 786436
  209.5 172.4 %copy-start.2 = (bf16[64,2048]{1,0:T(8,128)(2,1)S(1)}, bf16[64,2048]{1,0:T(8,128)(2,1)}, u32[]{:S(2)}) copy-start(bf16[64,2048]{1,0:T(8,128)(2,1)} %multiply_convert_fusion) | copy-start | bytes 786436
  209.5 170.7 %all-reduce.5.cloned.1.call-start = ((), (), s32[]{:S(2)}) async-start(), calls=%async_computation.5 | async-start | bytes 524288 | tf_op jit(solution)/shard_map/psum | solution.py:70
  363.2 119.9 %reduce-scatter.2.cloned.1.call-start = ((), (), s32[]{:S(2)}) async-start(), calls=%async_computation.4 | async-start | bytes 393216 | tf_op jit(solution)/shard_map/reduce_scatter | solution.py:98
Sparse Core Ops, SparseCore 0:
  10.8 115.5 all-gather.3
  208.8 71.9 all-gather.7
  284.1 74.6 all-gather.5
  363.3 16.9 all-reduce.4
  479.6 3.5 reduce-scatter.1
where the time goes:
time: 493 us; the launch traced here: 492 us
  waiting for transfers between devices  278 us (56%)
  blocking collectives  152 us (31%)
  matrix products  34.9 us (7%)
  between operations  15.6 us (3%)
  other arithmetic  10.6 us (2%)
    all_gather x1, waiting for transfers between devices, on_device(): piece = lax.all_gather(proj_weight, 'dp', axis=0, tiled=True)  118 us
    psum x1, blocking collectives, on_device(): lax.psum((jnp.sum(grad_na, axis=0), jnp.sum(grad_na * za, axis=0), jnp.su...  78.2 us
    psum x1, blocking collectives, on_device(): lax.psum((jnp.sum(values_a, axis=0), jnp.sum(values_a * values_a, axis=0)...  74 us
    all_gather x1, waiting for transfers between devices, on_device(): lax.all_gather(outgoing_a, 'dp', axis=0, tiled=True)  73.7 us
    all_gather x1, waiting for transfers between devices, on_device(): lax.all_gather(outgoing_b, 'dp', axis=0, tiled=True)  71.2 us
    dot_general x4, matrix products, contract_last(): lax.dot_general(left, right, (((1,), (1,)), ((), ())), preferred_element_...  21.5 us
    psum x1, waiting for transfers between devices, on_device(): lax.psum(contract_last(norm_b, whole_b).astype(jnp.bfloat16), 'tile')  11.2 us
  transfers between devices with their start and end apart: 5, of which 5 were waited for; matrix products, arithmetic and copies ran while one was open for 2% of the time, Pallas kernels for 0%

commit v1 on v0

--- a/solution.py
+++ b/solution.py
@@ -1,6 +1,11 @@
+import functools
+import itertools
+
 import jax
 import jax.numpy as jnp
 from jax import lax
+from jax.experimental import pallas as pl
+from jax.experimental.pallas import tpu as pltpu
 from jax.sharding import PartitionSpec as P
 
 EMB = 4096
@@ -101,9 +106,284 @@
     return (feats_grad, diag_corr, cross_power)
 
 
+ZS = 4
+QS = 4
+BF, F32 = jnp.bfloat16, jnp.float32
+
+
+def fused_kernel(
+    feats, jitter, mask, weight, out, diag_out, cross_out,
+    views, ids, wbuf, raw, norm, gpart, gsib, gsend, grecv, gfull,
+    small, sums, last, fsib_out, fsib, fown, fsend, frecv, send, recv, *, emb
+):
+    dp, t = lax.axis_index("dp"), lax.axis_index("tile")
+    rows, width = feats.shape
+    depth, local = weight.shape
+    cols = local // ZS
+    half = width // 2
+    batch = rows * ZS * QS
+    z, q = dp // QS, lax.rem(dp, QS)
+    x, y = lax.rem(q, 2), q // 2
+    sibling = (dp, 1 - t)
+    beside_x = (dp + 1 - 2 * x, t)
+    beside_y = (dp + 2 - 4 * y, t)
+    across = (dp + 1 - 2 * x + 2 - 4 * y, t)
+    q_x, q_y = q + 1 - 2 * x, q + 2 - 4 * y
+    other_z = [lax.rem(z + d, ZS) for d in range(ZS)]
+    from_z = [lax.rem(z + ZS - d, ZS) for d in range(ZS)]
+    at_z = [(other_z[d] * QS + q, t) for d in range(ZS)]
+    numbers = itertools.count()
+    started = []
+
+    def push(src, dst, device):
+        i = next(numbers)
+        copy = pltpu.make_async_remote_copy(
+            src_ref=src, dst_ref=dst, send_sem=send.at[i], recv_sem=recv.at[i],
+            device_id=device, device_id_type=pl.DeviceIdType.MESH,
+        )
+        copy.start()
+        started.append(copy)
+        return copy
+
+    barrier = pltpu.get_barrier_semaphore()
+    peers = [sibling, beside_x, beside_y, across] + at_z[1:]
+    for peer in peers:
+        pl.semaphore_signal(barrier, inc=1, device_id=peer, device_id_type=pl.DeviceIdType.MESH)
+    pl.semaphore_wait(barrier, len(peers))
+
+    def columns(d):
+        return pl.ds(pl.multiple_of(other_z[d] * cols, 128), cols)
+
+    w_z = {d: push(weight.at[:, columns(d)], wbuf.at[dp], at_z[d]) for d in (2, 1, 3)}
+    wbuf[dp] = weight[:, columns(0)]
+
+    group = lax.broadcasted_iota(jnp.int32, (rows, width), 1) // (width // GROUPS)
+    keep_a, keep_b = (group != mask[:, 0:1]), (group != mask[:, 1:2])
+    values = feats[...].astype(F32)
+    own = pl.ds(pl.multiple_of(z * rows, rows), rows)
+    views[0, own] = jnp.where(keep_a, values, 0.0).astype(BF)
+    views[1, own] = (jnp.where(keep_b, values, 0.0) + jitter[...].astype(F32)).astype(BF)
+    lanes = lax.broadcasted_iota(jnp.int32, (rows, 128), 1)
+    ids[own] = jnp.where(lanes < 64, mask[:, 0:1], mask[:, 1:2]).astype(F32)
+
+    def block(i):
+        return pl.ds(pl.multiple_of(i * rows, rows), rows)
+
+    mine = pl.ds(pl.multiple_of(t * half, 128), half)
+
+    def spread_weight(zz):
+        piece = wbuf.at[zz * QS + q]
+        return push(piece, piece, beside_x), push(piece, piece, beside_y), zz
+
+    first = [spread_weight(z)]
+    v_z = {d: push(views.at[:, own, mine], views.at[:, own, mine], at_z[d]) for d in (2, 1, 3)}
+    m_z = {d: push(ids.at[own], ids.at[own], at_z[d]) for d in (1, 2, 3)}
+    for d in (1, 3, 2):
+        w_z[d].wait_recv()
+        first.append(spread_weight(from_z[d]))
+    second = []
+    for via_x, via_y, zz in first:
+        via_x.wait_recv()
+        piece = wbuf.at[zz * QS + q_x, pl.ds(0, depth // 2)]
+        second.append(push(piece, piece, beside_y))
+        via_y.wait_recv()
+        piece = wbuf.at[zz * QS + q_y, pl.ds(depth // 2, depth // 2)]
+        second.append(push(piece, piece, beside_x))
+    v_s = []
+    for d in (1, 3, 2):
+        v_z[d].wait_recv()
+        piece = views.at[:, block(from_z[d]), mine]
+        v_s.append(push(piece, piece, sibling))
+    for copy in second + v_s:
+        copy.wait_recv()
+
+    raw_copies = []
+    for v in range(2):
+        flat = wbuf[...].reshape(width, cols)
+        raw[v, q] = jnp.dot(views[v], flat, preferred_element_type=F32).astype(BF)
+        piece = raw.at[v, q]
+        raw_copies.append((push(piece, piece, beside_x), push(piece, piece, beside_y)))
+    many = ZS * rows
+    second = []
+    for v in range(2):
+        raw_copies[v][0].wait_recv()
+        piece = raw.at[v, q_x, pl.ds(0, many // 2)]
+        second.append(push(piece, piece, beside_y))
+        raw_copies[v][1].wait_recv()
+        piece = raw.at[v, q_y, pl.ds(many // 2, many // 2)]
+        second.append(push(piece, piece, beside_x))
+    inverse = []
+    for v in range(2):
+        second[2 * v].wait_recv()
+        second[2 * v + 1].wait_recv()
+        total = jnp.zeros((1, cols), F32)
+        for i in range(QS):
+            total += jnp.sum(raw[v, i].astype(F32), axis=0, keepdims=True)
+        mean = total / batch
+        total = jnp.zeros((1, cols), F32)
+        for i in range(QS):
+            centered = raw[v, i].astype(F32) - mean
+            total += jnp.sum(centered * centered, axis=0, keepdims=True)
+        inv = lax.rsqrt(total / batch + NORM_EPS)
+        inverse.append(inv)
+        for i in range(QS):
+            norm[v, i] = ((raw[v, i].astype(F32) - mean) * inv).astype(BF)
+        gram = contract_last(norm[v, q], norm[v].reshape(batch, cols)).astype(BF)
+        for i in range(ZS):
+            for core in range(2):
+                start = i * rows + core * (rows // 2)
+                gpart[core, v, i] = gram[start : start + rows // 2]
+    g_s = push(gpart.at[1 - t], gsib, sibling)
+    total = jnp.zeros((1, cols), F32)
+    for i in range(QS):
+        total += jnp.sum(norm[0, i].astype(F32) * norm[1, i].astype(F32), axis=0, keepdims=True)
+    diag = total / batch
+    coeff = -2.0 * (1.0 - diag) - 2.0 * LAMBDA_OFF * diag
+    g_s.wait_recv()
+    g_z = {}
+    for d in (2, 1, 3, 0):
+        pair = gpart[t, :, other_z[d]].astype(F32) + gsib[:, other_z[d]].astype(F32)
+        if d:
+            gsend[d - 1] = pair.astype(BF)
+            g_z[d] = push(gsend.at[d - 1], grecv.at[d - 1], at_z[d])
+        else:
+            gram = pair
+    for d in (1, 3, 2):
+        g_z[d].wait_recv()
+        gram = gram + grecv[d - 1].astype(F32)
+    gfull[z, t] = gram.astype(BF)
+    piece = gfull.at[z, t]
+    g_z = {d: push(piece, piece, at_z[d]) for d in (2, 1, 3)}
+    g_s = [push(piece, piece, sibling)]
+    power = jnp.sum(gram[0] * gram[1], keepdims=True)
+    small[z] = jnp.concatenate(
+        [diag, jnp.broadcast_to(power, (1, cols)), jnp.zeros((6, cols), F32)], axis=0
+    )
+    small_z = {d: push(small.at[z], small.at[z], at_z[d]) for d in (1, 2, 3)}
+    for d in (1, 3, 2):
+        g_z[d].wait_recv()
+        piece = gfull.at[from_z[d], t]
+        g_s.append(push(piece, piece, sibling))
+    for copy in g_s:
+        copy.wait_recv()
+
+    factor = 2.0 * LAMBDA_OFF / (batch * batch)
+    za, zb = norm[0, q].astype(F32), norm[1, q].astype(F32)
+    gram_a = gfull[:, :, 0].reshape(many, batch)
+    gram_b = gfull[:, :, 1].reshape(many, batch)
+    grad_a = zb * (coeff / batch) + factor * jnp.dot(
+        gram_b, norm[0].reshape(batch, cols), preferred_element_type=F32
+    )
+    grad_b = za * (coeff / batch) + factor * jnp.dot(
+        gram_a, norm[1].reshape(batch, cols), preferred_element_type=F32
+    )
+    for d in (1, 2, 3):
+        small_z[d].wait_recv()
+    power = small[0, 1:2]
+    for i in range(1, ZS):
+        power = power + small[i, 1:2]
+    parts = [grad_a, grad_a * za, grad_b, grad_b * zb]
+    parts = [jnp.sum(part, axis=0, keepdims=True) for part in parts]
+    sums[q] = jnp.concatenate(parts + [power, jnp.zeros((3, cols), F32)], axis=0)
+    copies = [push(sums.at[q], sums.at[q], peer) for peer in (across, beside_x, beside_y)]
+    for i in range(ZS):
+        diag_out[0:1, i * cols : (i + 1) * cols] = small[i, 0:1]
+    for copy in copies:
+        copy.wait_recv()
+    total = sums[0]
+    for i in range(1, QS):
+        total = total + sums[i]
+    last[0] = total
+    last_copy = push(last.at[0], last.at[1], sibling)
+    mean = total / batch
+    dz_a = (inverse[0] * (grad_a - mean[0:1] - za * mean[1:2])).astype(BF)
+    dz_b = (inverse[1] * (grad_b - mean[2:3] - zb * mean[3:4])).astype(BF)
+
+    for d in (1, 2, 3):
+        m_z[d].wait_recv()
+
+    def share(core):
+        slabs = wbuf.shape[0] // 2
+        part = wbuf[pl.ds(core * slabs, slabs)].reshape(half, cols)
+        group = (lax.broadcasted_iota(jnp.int32, (1, half), 1) + core * half) // (width // GROUPS)
+        group = group.astype(F32)
+        back_a = jnp.where(group != ids[:, 0:1], contract_last(dz_a, part), 0.0)
+        return back_a + jnp.where(group != ids[:, 64:65], contract_last(dz_b, part), 0.0)
+
+    fsib_out[...] = share(1 - t).astype(BF).reshape(ZS, rows, half)
+    f_s = push(fsib_out, fsib, sibling)
+    fown[...] = share(t).reshape(ZS, rows, half)
+    f_s.wait_recv()
+    f_z = {}
+    for d in (2, 1, 3, 0):
+        pair = fown[other_z[d]] + fsib[other_z[d]].astype(F32)
+        if d:
+            fsend[d - 1] = pair.astype(BF)
+            f_z[d] = push(fsend.at[d - 1], frecv.at[d - 1], at_z[d])
+        else:
+            result = pair
+    last_copy.wait_recv()
+    power = last[0, 4:5, 0:128] + last[1, 4:5, 0:128]
+    cross_out[...] = jnp.broadcast_to(power, (8, 128)) / (batch * batch) / emb
+    for d in (1, 3, 2):
+        f_z[d].wait_recv()
+        result = result + frecv[d - 1].astype(F32)
+    out[...] = LOSS_SCALE * result
+    for copy in started:
+        copy.wait_send()
+
+
+COPIES = 80
+
+
+def fused(feats, jitter, mask_ids, proj_weight):
+    rows, width = feats.shape
+    depth, local = proj_weight.shape
+    cols, half, many = local // ZS, width // 2, rows * ZS
+    batch = many * QS
+    vmem = pl.BlockSpec(memory_space=pltpu.VMEM)
+    grad, diag, power = pl.pallas_call(
+        functools.partial(fused_kernel, emb=EMB),
+        out_shape=(
+            jax.ShapeDtypeStruct((rows, half), F32),
+            jax.ShapeDtypeStruct((1, local), F32),
+            jax.ShapeDtypeStruct((8, 128), F32),
+        ),
+        in_specs=[vmem] * 4,
+        out_specs=(vmem,) * 3,
+        scratch_shapes=[
+            pltpu.VMEM((2, many, width), BF),
+            pltpu.VMEM((many, 128), F32),
+            pltpu.VMEM((ZS * QS, depth, cols), BF),
+            pltpu.VMEM((2, QS, many, cols), BF),
+            pltpu.VMEM((2, QS, many, cols), BF),
+            pltpu.VMEM((2, 2, ZS, rows // 2, batch), BF),
+            pltpu.VMEM((2, ZS, rows // 2, batch), BF),
+            pltpu.VMEM((ZS - 1, 2, rows // 2, batch), BF),
+            pltpu.VMEM((ZS - 1, 2, rows // 2, batch), BF),
+            pltpu.VMEM((ZS, 2, 2, rows // 2, batch), BF),
+            pltpu.VMEM((ZS, 8, cols), F32),
+            pltpu.VMEM((QS, 8, cols), F32),
+            pltpu.VMEM((2, 8, cols), F32),
+            pltpu.VMEM((ZS, rows, half), BF),
+            pltpu.VMEM((ZS, rows, half), BF),
+            pltpu.VMEM((ZS, rows, half), F32),
+            pltpu.VMEM((ZS - 1, rows, half), BF),
+            pltpu.VMEM((ZS - 1, rows, half), BF),
+            pltpu.SemaphoreType.DMA((COPIES,)),
+            pltpu.SemaphoreType.DMA((COPIES,)),
+        ],
+        compiler_params=pltpu.CompilerParams(
+            collective_id=0, has_side_effects=True, vmem_limit_bytes=56 * 2**20
+        ),
+    )(feats, jitter, mask_ids, proj_weight)
+    return grad, diag.reshape(local), power[0, 0]
+
+
 def solution(mesh):
     in_specs = (P("dp", None), P("dp", None), P("dp", None), P("dp", "tile"))
     out_specs = (P("dp", "tile"), P("tile"), P())
+    planes = mesh.shape["dp"] == ZS * QS and mesh.shape["tile"] == 2
     return jax.shard_map(
-        on_device, mesh=mesh, in_specs=in_specs, out_specs=out_specs, check_vma=False
-    )
+        fused if planes else on_device, mesh=mesh, in_specs=in_specs, out_specs=out_specs, check_vma=False
+    )

time: 493 us -> 116 us (0.24)
  waiting for transfers between devices: 278 us -> 0 us
  blocking collectives: 152 us -> 0 us
  Pallas kernels: 0 us -> 110 us
  matrix products: 34.9 us -> 0 us
  between operations: 15.6 us -> 0.64 us
  other arithmetic: 10.6 us -> 0 us
    all_gather x3 -> x0, waiting for transfers between devices: 263 us -> none  [the longest x1 118 us: on_device(): piece = lax.all_gather(proj_weight, 'dp', axis=0, tiled=True)]
    psum x2 -> x0, blocking collectives: 152 us -> none  [the longest x1 78.2 us: on_device(): lax.psum((jnp.sum(grad_na, axis=0), jnp.sum(grad_na * za, axis=0), jnp.su...]
    pallas_call x0 -> x1, Pallas kernels: none -> 110 us  [fused(): pl.pallas_call(functools.partial(fused_kernel, emb=EMB), out_shape=(jax.S...]
    dot_general x8 -> x0, matrix products: 34.9 us -> none  [the longest x4 21.5 us: contract_last(): lax.dot_general(left, right, (((1,), (1,)), ((), ())), preferred_element_...]
    psum x1 -> x0, waiting for transfers between devices: 11.2 us -> none  [on_device(): lax.psum(contract_last(norm_b, whole_b).astype(jnp.bfloat16), 'tile')]
    reduce_sum x2 -> x0, other arithmetic: 6.85 us -> none  [the longest x1 5.21 us: on_device(): jnp.sum(whole_a.astype(jnp.float32) * whole_b.astype(jnp.float32), axis=0)]
  transfers between devices with their start and end apart: 5 -> 0, of which waited for: 5 -> 0; matrix products, arithmetic and copies ran while one was open for 2% -> 0% of each run, Pallas kernels for 0% -> 0%
where the time goes in v1:
time: 116 us
  Pallas kernels  110 us (95%)
  local copies, waits for them, and re-layouts  4.86 us (4%)
    pallas_call x1, Pallas kernels, fused(): pl.pallas_call(functools.partial(fused_kernel, emb=EMB), out_shape=(jax.S...  110 us
    unnamed x5, local copies, waits for them, and re-layouts  3.67 us

profile of v1, /device:TPU:0, one launch (start us, length us, event | category | flops | bytes accessed | tf_op | source)
XLA Modules:
  0.0 115.6 jit_solution(177658056450776759)
XLA Ops:
  0.6 1.4 %copy.7.mask = s32[64,2]{1,0:T(8,128)} copy(s32[64,2]{0,1:T(2,128)} %param.6) | data formatting | bytes 1024 | tf_op args[2]
  2.0 110.1 %shard_map.67 = (f32[64,1024]{1,0:T(8,128)}, f32[1,2048]{1,0:T(1,128)}, f32[8,128]{1,0:T(8,128)}) custom-call(bf16[64,2048]{1,0:T(8,128)(2,1)} %feats.1, bf16[64,2048]{1,0:T(8,128)(2,1)} %jitter.1, s32[64,2]{1,0:T(8,128)} %copy.7.mask, bf16[128,2048]{1,0:T(8,128)(2,1)} %weight.1), custom_call_target="tpu_custom_call" | custom-call | tf_op jit(solution)/shard_map/pallas_call | solution.py:345
  112.1 1.2 %slice.3 = f32[1,1]{1,0:T(1,128)} slice(f32[8,128]{1,0:T(8,128)} %get-tuple-element.8), slice={[0:1], [0:1]} | slice | bytes 8 | tf_op jit(solution)/shard_map/slice | solution.py:380
  113.3 0.0 copy-start
  113.3 1.7 %copy.10 = f32[64,1024]{1,0:T(8,128)} copy(f32[64,1024]{1,0:T(8,128)} %get-tuple-element.12) | data formatting | bytes 524288
  115.0 0.0 copy-done
  115.0 0.6 copy.11
Async XLA Ops:
  113.3 1.7 %copy-start = (f32[1,2048]{1,0:T(1,128)S(1)}, f32[1,2048]{1,0:T(1,128)}, u32[]{:S(2)}) copy-start(f32[1,2048]{1,0:T(1,128)} %get-tuple-element.7) | copy-start | bytes 24580

commit v2 on v0

--- a/solution.py
+++ b/solution.py
@@ -1,6 +1,11 @@
+import functools
+import itertools
+
 import jax
 import jax.numpy as jnp
 from jax import lax
+from jax.experimental import pallas as pl
+from jax.experimental.pallas import tpu as pltpu
 from jax.sharding import PartitionSpec as P
 
 EMB = 4096
@@ -101,9 +106,365 @@
     return (feats_grad, diag_corr, cross_power)
 
 
+ZS = 4
+QS = 4
+BF, F32 = jnp.bfloat16, jnp.float32
+
+
+def fused_kernel(
+    feats, jitter, mask, weight, out, diag_out, cross_out,
+    views, ids, wbuf, raw, norm, gpart, gsib, gsend, grecv, gsum, gfull,
+    stat, small, sums, last, fsib_out, fsib, fown, fsend, frecv, send, recv, *, emb
+):
+    dp, t = lax.axis_index("dp"), lax.axis_index("tile")
+    rows, width = feats.shape
+    depth, local = weight.shape
+    cols = local // ZS
+    half = width // 2
+    batch = rows * ZS * QS
+    z, q = dp // QS, lax.rem(dp, QS)
+    x, y = lax.rem(q, 2), q // 2
+    sibling = (dp, 1 - t)
+    beside_x = (dp + 1 - 2 * x, t)
+    beside_y = (dp + 2 - 4 * y, t)
+    across = (dp + 1 - 2 * x + 2 - 4 * y, t)
+    q_x, q_y = q + 1 - 2 * x, q + 2 - 4 * y
+    other_z = [lax.rem(z + d, ZS) for d in range(ZS)]
+    from_z = [lax.rem(z + ZS - d, ZS) for d in range(ZS)]
+    at_z = [(other_z[d] * QS + q, t) for d in range(ZS)]
+    numbers = itertools.count()
+    started = []
+
+    def push(src, dst, device):
+        i = next(numbers)
+        copy = pltpu.make_async_remote_copy(
+            src_ref=src, dst_ref=dst, send_sem=send.at[i], recv_sem=recv.at[i],
+            device_id=device, device_id_type=pl.DeviceIdType.MESH,
+        )
+        copy.start()
+        started.append(copy)
+        return copy
+
+    barrier = pltpu.get_barrier_semaphore()
+    peers = [sibling, beside_x, beside_y, across] + at_z[1:]
+    for peer in peers:
+        pl.semaphore_signal(barrier, inc=1, device_id=peer, device_id_type=pl.DeviceIdType.MESH)
+
+    def block(i):
+        return pl.ds(pl.multiple_of(i * rows, rows), rows)
+
+    own = block(z)
+    mine = pl.ds(pl.multiple_of(t * half, 128), half)
+
+    square = [lax.broadcasted_iota(jnp.int32, (rows, rows), axis) for axis in range(2)]
+
+    def id_column(v):
+        row = jnp.broadcast_to(mask[v : v + 1, :].astype(F32), (rows, rows))
+        return jnp.sum(jnp.where(square[0] == square[1], row, 0.0), axis=1, keepdims=True)
+
+    id_a, id_b = id_column(0), id_column(1)
+    group = lax.broadcasted_iota(jnp.int32, (1, width), 1) // (width // GROUPS)
+    group = group.astype(F32)
+    values = feats[...].astype(F32)
+    views[0, own] = jnp.where(group != id_a, values, 0.0).astype(BF)
+    views[1, own] = (jnp.where(group != id_b, values, 0.0) + jitter[...].astype(F32)).astype(BF)
+    lanes = lax.broadcasted_iota(jnp.int32, (rows, 128), 1)
+    ids[own] = jnp.where(lanes < 64, id_a, id_b)
+
+    def columns(d):
+        return pl.ds(pl.multiple_of(other_z[d] * cols, 128), cols)
+
+    wbuf[dp] = weight[:, columns(0)]
+    pl.semaphore_wait(barrier, len(peers))
+    w_z = {d: push(weight.at[:, columns(d)], wbuf.at[dp], at_z[d]) for d in (2, 1, 3)}
+
+    def spread_weight(zz):
+        piece = wbuf.at[zz * QS + q]
+        return push(piece, piece, beside_x), push(piece, piece, beside_y), zz
+
+    first = [spread_weight(z)]
+    v_z = {}
+    for v in range(2):
+        for d in (1, 3, 2):
+            piece = views.at[v, own, mine]
+            v_z[v, d] = push(piece, piece, at_z[d])
+    m_z = {d: push(ids.at[own], ids.at[own], at_z[d]) for d in (1, 2, 3)}
+    second = []
+
+    def forward_weight(entry):
+        via_x, via_y, zz = entry
+        via_x.wait_recv()
+        piece = wbuf.at[zz * QS + q_x, pl.ds(0, depth // 2)]
+        second.append(push(piece, piece, beside_y))
+        via_y.wait_recv()
+        piece = wbuf.at[zz * QS + q_y, pl.ds(depth // 2, depth // 2)]
+        second.append(push(piece, piece, beside_x))
+
+    for d in (1, 3, 2):
+        w_z[d].wait_recv()
+        first.append(spread_weight(from_z[d]))
+        forward_weight(first[-2])
+    forward_weight(first[-1])
+
+    steps = [(v, d) for v in range(2) for d in (0, 1, 3, 2)]
+    v_s, raw_copies, crossed, stat_copies = {}, {}, {0: [], 1: []}, {}
+    many = ZS * rows
+
+    def share_view(v, d):
+        if d:
+            v_z[v, d].wait_recv()
+            piece = views.at[v, block(from_z[d]), mine]
+            v_s[v, d] = push(piece, piece, sibling)
+
+    def project(v, d):
+        if d:
+            v_s[v, d].wait_recv()
+        there = block(from_z[d])
+        flat = wbuf[...].reshape(width, cols)
+        raw[v, q, there] = jnp.dot(views[v, there], flat, preferred_element_type=F32).astype(BF)
+        piece = raw.at[v, q, there]
+        raw_copies[v, d] = push(piece, piece, beside_x), push(piece, piece, beside_y)
+
+    def forward_raw(v, d):
+        start = pl.multiple_of(from_z[d] * rows, rows)
+        raw_copies[v, d][0].wait_recv()
+        piece = raw.at[v, q_x, pl.ds(start, rows // 2)]
+        crossed[v].append(push(piece, piece, beside_y))
+        raw_copies[v, d][1].wait_recv()
+        piece = raw.at[v, q_y, pl.ds(pl.multiple_of(start + rows // 2, rows // 2), rows // 2)]
+        crossed[v].append(push(piece, piece, beside_x))
+
+    def moments(v):
+        held = raw[v, q].astype(F32)
+        mean = jnp.sum(held, axis=0, keepdims=True) / many
+        held = held - mean
+        spread = jnp.sum(held * held, axis=0, keepdims=True)
+        stat[v, q] = jnp.concatenate([mean, spread, jnp.zeros((6, cols), F32)], axis=0)
+        piece = stat.at[v, q]
+        stat_copies[v] = [push(piece, piece, peer) for peer in (across, beside_x, beside_y)]
+
+    share_view(*steps[0])
+    share_view(*steps[1])
+    for copy in second:
+        copy.wait_recv()
+    for i, step in enumerate(steps):
+        project(*step)
+        if i + 2 < len(steps):
+            share_view(*steps[i + 2])
+        if step[1] == 2:
+            moments(step[0])
+        if i:
+            forward_raw(*steps[i - 1])
+
+    inverse = {}
+
+    def gram_part(v):
+        for copy in stat_copies[v]:
+            copy.wait_recv()
+        mean = stat[v, 0, 0:1]
+        for i in range(1, QS):
+            mean = mean + stat[v, i, 0:1]
+        mean = mean / QS
+        total = jnp.zeros((1, cols), F32)
+        for i in range(QS):
+            off = stat[v, i, 0:1] - mean
+            total = total + stat[v, i, 1:2] + many * (off * off)
+        inv = lax.rsqrt(total / batch + NORM_EPS)
+        inverse[v] = inv
+        for k, source in enumerate((q, q_x, q_y, QS - 1 - q)):
+            if k == QS - 1:
+                for copy in crossed[v]:
+                    copy.wait_recv()
+            norm[v, source] = ((raw[v, source].astype(F32) - mean) * inv).astype(BF)
+            gram = contract_last(norm[v, q], norm[v, source]).astype(BF)
+            lane = pl.ds(pl.multiple_of(source * many, 128), many)
+            for i in range(ZS):
+                for core in range(2):
+                    start = i * rows + core * (rows // 2)
+                    gpart[v, core, i, :, lane] = gram[start : start + rows // 2]
+        return push(gpart.at[v, 1 - t], gsib.at[v], sibling)
+
+    def gram_scatter(v, copy):
+        copy.wait_recv()
+        copies = {}
+        for d in (2, 1, 3):
+            pair = gpart[v, t, other_z[d]].astype(F32) + gsib[v, other_z[d]].astype(F32)
+            gsend[v, d - 1] = pair.astype(BF)
+            copies[d] = push(gsend.at[v, d - 1], grecv.at[v, d - 1], at_z[d])
+        gsum[v] = gpart[v, t, z].astype(F32) + gsib[v, z].astype(F32)
+        return copies
+
+    def gram_sum(v, copies):
+        gram = gsum[v]
+        for d in (1, 3, 2):
+            copies[d].wait_recv()
+            gram = gram + grecv[v, d - 1].astype(F32)
+        gsum[v] = gram
+        gfull[v, z, t] = gram.astype(BF)
+        piece = gfull.at[v, z, t]
+        return {d: push(piece, piece, at_z[d]) for d in (2, 1, 3)}, [push(piece, piece, sibling)]
+
+    def gram_share(v, along, within):
+        for d in (1, 3, 2):
+            along[d].wait_recv()
+            piece = gfull.at[v, from_z[d], t]
+            within.append(push(piece, piece, sibling))
+
+    factor = 2.0 * LAMBDA_OFF / (batch * batch)
+
+    def grad_of(v, slot, extra):
+        here, other = norm[v, q].astype(F32), norm[1 - v, q].astype(F32)
+        grad = other * (coeff / batch) + factor * jnp.dot(
+            gfull[1 - v].reshape(many, batch), norm[v].reshape(batch, cols),
+            preferred_element_type=F32,
+        )
+        parts = [jnp.sum(part, axis=0, keepdims=True) for part in (grad, grad * here)]
+        sums[slot, q] = jnp.concatenate(parts + extra + [jnp.zeros((6 - len(extra), cols), F32)], axis=0)
+        piece = sums.at[slot, q]
+        return grad, [push(piece, piece, peer) for peer in (across, beside_x, beside_y)]
+
+    def summed(slot, copies):
+        for copy in copies:
+            copy.wait_recv()
+        total = sums[slot, 0]
+        for i in range(1, QS):
+            total = total + sums[slot, i]
+        return total
+
+    def norm_back(v, grad, total):
+        mean = total / batch
+        here = norm[v, q].astype(F32)
+        return (inverse[v] * (grad - mean[0:1] - here * mean[1:2])).astype(BF)
+
+    sib_a = gram_part(0)
+    forward_raw(*steps[-1])
+    z_a = gram_scatter(0, sib_a)
+    sib_b = gram_part(1)
+    along_a, within_a = gram_sum(0, z_a)
+    z_b = gram_scatter(1, sib_b)
+    total = jnp.zeros((1, cols), F32)
+    for i in range(QS):
+        total += jnp.sum(norm[0, i].astype(F32) * norm[1, i].astype(F32), axis=0, keepdims=True)
+    diag = total / batch
+    coeff = -2.0 * (1.0 - diag) - 2.0 * LAMBDA_OFF * diag
+    gram_share(0, along_a, within_a)
+    along_b, within_b = gram_sum(1, z_b)
+    power = jnp.sum(gsum[0] * gsum[1], keepdims=True)
+    small[z] = jnp.concatenate(
+        [diag, jnp.broadcast_to(power, (1, cols)), jnp.zeros((6, cols), F32)], axis=0
+    )
+    small_z = {d: push(small.at[z], small.at[z], at_z[d]) for d in (1, 2, 3)}
+    for copy in within_a:
+        copy.wait_recv()
+    grad, copies = grad_of(1, 0, [])
+    for d in (1, 2, 3):
+        m_z[d].wait_recv()
+    dz_b = norm_back(1, grad, summed(0, copies))
+    slabs = wbuf.shape[0] // 4
+    chunk = half // 2
+
+    def back(dz, core, c, lane):
+        part = wbuf[pl.ds((core * 2 + c) * slabs, slabs)].reshape(chunk, cols)
+        group = lax.broadcasted_iota(jnp.int32, (1, chunk), 1) + (core * 2 + c) * chunk
+        group = (group // (width // GROUPS)).astype(F32)
+        return jnp.where(group != ids[:, lane : lane + 1], contract_last(dz, part), 0.0)
+
+    order = [(1 - t, 0), (1 - t, 1), (t, 0), (t, 1)]
+    gram_share(1, along_b, within_b)
+    for i, (core, c) in enumerate(order):
+        fown[i] = back(dz_b, core, c, 64)
+    for copy in within_b:
+        copy.wait_recv()
+    for d in (1, 2, 3):
+        small_z[d].wait_recv()
+    power = small[0, 1:2]
+    for i in range(1, ZS):
+        power = power + small[i, 1:2]
+        diag_out[0:1, i * cols : (i + 1) * cols] = small[i, 0:1]
+    diag_out[0:1, 0:cols] = small[0, 0:1]
+    grad, copies = grad_of(0, 1, [power])
+    total = summed(1, copies)
+    last[0] = total
+    last_copy = push(last.at[0], last.at[1], sibling)
+    dz_a = norm_back(0, grad, total)
+
+    f_s, f_z = {}, {}
+    for c in range(2):
+        fsib_out[c] = (fown[c] + back(dz_a, 1 - t, c, 0)).astype(BF).reshape(ZS, rows, chunk)
+        f_s[c] = push(fsib_out.at[c], fsib.at[c], sibling)
+    for c in range(2):
+        pair = fown[2 + c] + back(dz_a, t, c, 0)
+        f_s[c].wait_recv()
+        fown[2 + c] = pair + fsib[c].astype(F32).reshape(many, chunk)
+        for d in (2, 1, 3):
+            fsend[c, d - 1] = fown[2 + c, block(other_z[d])].astype(BF)
+            f_z[c, d] = push(fsend.at[c, d - 1], frecv.at[c, d - 1], at_z[d])
+    last_copy.wait_recv()
+    power = last[0, 2:3, 0:1] + last[1, 2:3, 0:1]
+    cross_out[...] = power / (batch * batch) / emb
+    for c in range(2):
+        result = fown[2 + c, own]
+        for d in (1, 3, 2):
+            f_z[c, d].wait_recv()
+            result = result + frecv[c, d - 1].astype(F32)
+        out[:, c * chunk : (c + 1) * chunk] = LOSS_SCALE * result
+    for copy in started:
+        copy.wait_send()
+
+
+COPIES = 128
+
+
+def fused(feats, jitter, mask_ids, proj_weight):
+    rows, width = feats.shape
+    depth, local = proj_weight.shape
+    cols, half, many = local // ZS, width // 2, rows * ZS
+    batch = many * QS
+    vmem = pl.BlockSpec(memory_space=pltpu.VMEM)
+    grad, diag, power = pl.pallas_call(
+        functools.partial(fused_kernel, emb=EMB),
+        out_shape=(
+            jax.ShapeDtypeStruct((rows, half), F32),
+            jax.ShapeDtypeStruct((1, local), F32),
+            jax.ShapeDtypeStruct((1, 1), F32),
+        ),
+        in_specs=[vmem] * 4,
+        out_specs=(vmem,) * 3,
+        scratch_shapes=[
+            pltpu.VMEM((2, many, width), BF),
+            pltpu.VMEM((many, 128), F32),
+            pltpu.VMEM((ZS * QS, depth, cols), BF),
+            pltpu.VMEM((2, QS, many, cols), BF),
+            pltpu.VMEM((2, QS, many, cols), BF),
+            pltpu.VMEM((2, 2, ZS, rows // 2, batch), BF),
+            pltpu.VMEM((2, ZS, rows // 2, batch), BF),
+            pltpu.VMEM((2, ZS - 1, rows // 2, batch), BF),
+            pltpu.VMEM((2, ZS - 1, rows // 2, batch), BF),
+            pltpu.VMEM((2, rows // 2, batch), F32),
+            pltpu.VMEM((2, ZS, 2, rows // 2, batch), BF),
+            pltpu.VMEM((2, QS, 8, cols), F32),
+            pltpu.VMEM((ZS, 8, cols), F32),
+            pltpu.VMEM((2, QS, 8, cols), F32),
+            pltpu.VMEM((2, 8, cols), F32),
+            pltpu.VMEM((2, ZS, rows, half // 2), BF),
+            pltpu.VMEM((2, ZS, rows, half // 2), BF),
+            pltpu.VMEM((4, many, half // 2), F32),
+            pltpu.VMEM((2, ZS - 1, rows, half // 2), BF),
+            pltpu.VMEM((2, ZS - 1, rows, half // 2), BF),
+            pltpu.SemaphoreType.DMA((COPIES,)),
+            pltpu.SemaphoreType.DMA((COPIES,)),
+        ],
+        compiler_params=pltpu.CompilerParams(
+            collective_id=0, has_side_effects=True, vmem_limit_bytes=56 * 2**20
+        ),
+    )(feats, jitter, mask_ids.T, proj_weight)
+    return grad, diag.reshape(local), power.reshape(())
+
+
 def solution(mesh):
     in_specs = (P("dp", None), P("dp", None), P("dp", None), P("dp", "tile"))
     out_specs = (P("dp", "tile"), P("tile"), P())
+    planes = mesh.shape["dp"] == ZS * QS and mesh.shape["tile"] == 2
     return jax.shard_map(
-        on_device, mesh=mesh, in_specs=in_specs, out_specs=out_specs, check_vma=False
-    )
+        fused if planes else on_device, mesh=mesh, in_specs=in_specs, out_specs=out_specs, check_vma=False
+    )

time: 493 us -> 111 us (0.23)
  waiting for transfers between devices: 278 us -> 0 us
  blocking collectives: 152 us -> 0 us
  Pallas kernels: 0 us -> 106 us
  matrix products: 34.9 us -> 0 us
  between operations: 15.6 us -> 2.46 us
  other arithmetic: 10.6 us -> 0 us
    all_gather x3 -> x0, waiting for transfers between devices: 263 us -> none  [the longest x1 118 us: on_device(): piece = lax.all_gather(proj_weight, 'dp', axis=0, tiled=True)]
    psum x2 -> x0, blocking collectives: 152 us -> none  [the longest x1 78.2 us: on_device(): lax.psum((jnp.sum(grad_na, axis=0), jnp.sum(grad_na * za, axis=0), jnp.su...]
    pallas_call x0 -> x1, Pallas kernels: none -> 106 us  [fused(): pl.pallas_call(functools.partial(fused_kernel, emb=EMB), out_shape=(jax.S...]
    dot_general x8 -> x0, matrix products: 34.9 us -> none  [the longest x4 21.5 us: contract_last(): lax.dot_general(left, right, (((1,), (1,)), ((), ())), preferred_element_...]
    psum x1 -> x0, waiting for transfers between devices: 11.2 us -> none  [on_device(): lax.psum(contract_last(norm_b, whole_b).astype(jnp.bfloat16), 'tile')]
    reduce_sum x2 -> x0, other arithmetic: 6.85 us -> none  [the longest x1 5.21 us: on_device(): jnp.sum(whole_a.astype(jnp.float32) * whole_b.astype(jnp.float32), axis=0)]
  transfers between devices with their start and end apart: 5 -> 0, of which waited for: 5 -> 0; matrix products, arithmetic and copies ran while one was open for 2% -> 0% of each run, Pallas kernels for 0% -> 0%
where the time goes in v2:
time: 111 us
  Pallas kernels  106 us (95%)
  between operations  2.46 us (2%)
  local copies, waits for them, and re-layouts  2.28 us (2%)
    pallas_call x1, Pallas kernels, fused(): pl.pallas_call(functools.partial(fused_kernel, emb=EMB), out_shape=(jax.S...  106 us
    unnamed x4, local copies, waits for them, and re-layouts  2.28 us

profile of v2, /device:TPU:0, one launch (start us, length us, event | category | flops | bytes accessed | tf_op | source)
XLA Modules:
  0.0 110.6 jit_solution(7689310980066227708)
XLA Ops:
  0.6 105.8 %shard_map.67 = (f32[64,1024]{1,0:T(8,128)}, f32[1,2048]{1,0:T(1,128)}, f32[1,1]{1,0:T(1,128)}) custom-call(bf16[64,2048]{1,0:T(8,128)(2,1)} %feats.1, bf16[64,2048]{1,0:T(8,128)(2,1)} %jitter.1, s32[2,64]{1,0:T(2,128)} %bitcast.4, bf16[128,2048]{1,0:T(8,128)(2,1)} %weight.1), custom_call_target="tpu_custom_call" | custom-call | tf_op jit(solution)/shard_map/pallas_call | solution.py:424
  106.4 0.0 copy-start
  106.5 1.7 %copy.10 = f32[64,1024]{1,0:T(8,128)} copy(f32[64,1024]{1,0:T(8,128)} %get-tuple-element.12) | data formatting | bytes 524288
  108.1 0.0 copy-done
  108.1 0.6 copy.11
Async XLA Ops:
  106.4 1.7 %copy-start = (f32[1,2048]{1,0:T(1,128)S(1)}, f32[1,2048]{1,0:T(1,128)}, u32[]{:S(2)}) copy-start(f32[1,2048]{1,0:T(1,128)} %get-tuple-element.7) | copy-start | bytes 24580

commit v3 on v2

--- a/solution.py
+++ b/solution.py
@@ -114,7 +114,7 @@
 def fused_kernel(
     feats, jitter, mask, weight, out, diag_out, cross_out,
     views, ids, wbuf, raw, norm, gpart, gsib, gsend, grecv, gsum, gfull,
-    stat, small, sums, last, fsib_out, fsib, fown, fsend, frecv, send, recv, *, emb
+    stat, small, sums, last, fsib_out, fsib, fown, fsend, frecv, send, recv, hop_send, hop_recv, *, emb
 ):
     dp, t = lax.axis_index("dp"), lax.axis_index("tile")
     rows, width = feats.shape
@@ -183,11 +183,23 @@
         return push(piece, piece, beside_x), push(piece, piece, beside_y), zz
 
     first = [spread_weight(z)]
-    v_z = {}
+
+    sources = [z, z + 1 - 2 * lax.rem(z, 2), 2 - z // 2, (ZS - 1) * (1 - z // 2)]
+
+    def hop(v, source, up):
+        piece = views.at[v, block(source), mine]
+        return pltpu.make_async_remote_copy(
+            src_ref=piece, dst_ref=piece, send_sem=hop_send.at[v, up, source],
+            recv_sem=hop_recv.at[v, source], device_id=(dp + (QS if up else -QS), t),
+            device_id_type=pl.DeviceIdType.MESH,
+        )
+
+    def hop_on(v, source, act):
+        pl.when((source <= z) & (z < ZS - 1))(lambda: act(hop(v, source, 1)))
+        pl.when((source >= z) & (z > 0))(lambda: act(hop(v, source, 0)))
+
     for v in range(2):
-        for d in (1, 3, 2):
-            piece = views.at[v, own, mine]
-            v_z[v, d] = push(piece, piece, at_z[d])
+        hop_on(v, z, lambda copy: copy.start())
     m_z = {d: push(ids.at[own], ids.at[own], at_z[d]) for d in (1, 2, 3)}
     second = []
 
@@ -200,37 +212,32 @@
         piece = wbuf.at[zz * QS + q_y, pl.ds(depth // 2, depth // 2)]
         second.append(push(piece, piece, beside_x))
 
-    for d in (1, 3, 2):
-        w_z[d].wait_recv()
-        first.append(spread_weight(from_z[d]))
-        forward_weight(first[-2])
-    forward_weight(first[-1])
-
-    steps = [(v, d) for v in range(2) for d in (0, 1, 3, 2)]
+    steps = [(v, k) for v in range(2) for k in range(ZS)]
     v_s, raw_copies, crossed, stat_copies = {}, {}, {0: [], 1: []}, {}
     many = ZS * rows
 
-    def share_view(v, d):
-        if d:
-            v_z[v, d].wait_recv()
-            piece = views.at[v, block(from_z[d]), mine]
-            v_s[v, d] = push(piece, piece, sibling)
-
-    def project(v, d):
-        if d:
-            v_s[v, d].wait_recv()
-        there = block(from_z[d])
+    def share_view(v, k):
+        if k:
+            hop(v, sources[k], 1).wait_recv()
+            hop_on(v, sources[k], lambda copy: copy.start())
+            piece = views.at[v, block(sources[k]), mine]
+            v_s[v, k] = push(piece, piece, sibling)
+
+    def project(v, k):
+        if k:
+            v_s[v, k].wait_recv()
+        there = block(sources[k])
         flat = wbuf[...].reshape(width, cols)
         raw[v, q, there] = jnp.dot(views[v, there], flat, preferred_element_type=F32).astype(BF)
         piece = raw.at[v, q, there]
-        raw_copies[v, d] = push(piece, piece, beside_x), push(piece, piece, beside_y)
-
-    def forward_raw(v, d):
-        start = pl.multiple_of(from_z[d] * rows, rows)
-        raw_copies[v, d][0].wait_recv()
+        raw_copies[v, k] = push(piece, piece, beside_x), push(piece, piece, beside_y)
+
+    def forward_raw(v, k):
+        start = pl.multiple_of(sources[k] * rows, rows)
+        raw_copies[v, k][0].wait_recv()
         piece = raw.at[v, q_x, pl.ds(start, rows // 2)]
         crossed[v].append(push(piece, piece, beside_y))
-        raw_copies[v, d][1].wait_recv()
+        raw_copies[v, k][1].wait_recv()
         piece = raw.at[v, q_y, pl.ds(pl.multiple_of(start + rows // 2, rows // 2), rows // 2)]
         crossed[v].append(push(piece, piece, beside_x))
 
@@ -243,15 +250,28 @@
         piece = stat.at[v, q]
         stat_copies[v] = [push(piece, piece, peer) for peer in (across, beside_x, beside_y)]
 
-    share_view(*steps[0])
-    share_view(*steps[1])
+    w_z[1].wait_recv()
+    first.append(spread_weight(from_z[1]))
+    forward_weight(first[0])
+    for d in (3, 2):
+        w_z[d].wait_recv()
+        first.append(spread_weight(from_z[d]))
+    share_view(0, 1)
+    forward_weight(first[1])
+    share_view(0, 2)
+    forward_weight(first[2])
+    share_view(0, 3)
+    forward_weight(first[3])
+    share_view(1, 1)
     for copy in second:
         copy.wait_recv()
     for i, step in enumerate(steps):
         project(*step)
-        if i + 2 < len(steps):
-            share_view(*steps[i + 2])
-        if step[1] == 2:
+        if step == (0, 1):
+            share_view(1, 2)
+        if step == (0, 3):
+            share_view(1, 3)
+        if step[1] == ZS - 1:
             moments(step[0])
         if i:
             forward_raw(*steps[i - 1])
@@ -410,6 +430,9 @@
         out[:, c * chunk : (c + 1) * chunk] = LOSS_SCALE * result
     for copy in started:
         copy.wait_send()
+    for v in range(2):
+        for source in sources:
+            hop_on(v, source, lambda copy: copy.wait_send())
 
 
 COPIES = 128
@@ -453,6 +476,8 @@
             pltpu.VMEM((2, ZS - 1, rows, half // 2), BF),
             pltpu.SemaphoreType.DMA((COPIES,)),
             pltpu.SemaphoreType.DMA((COPIES,)),
+            pltpu.SemaphoreType.DMA((2, 2, ZS)),
+            pltpu.SemaphoreType.DMA((2, ZS)),
         ],
         compiler_params=pltpu.CompilerParams(
             collective_id=0, has_side_effects=True, vmem_limit_bytes=56 * 2**20

time: 111 us -> 112 us (level)
    pallas_call x1, Pallas kernels: 106 us -> 107 us  [fused(): pl.pallas_call(functools.partial(fused_kernel, emb=EMB), out_shape=(jax.S...]
where the time goes in v3:
time: 112 us
  Pallas kernels  107 us (96%)
  between operations  2.46 us (2%)
  local copies, waits for them, and re-layouts  2.28 us (2%)
    pallas_call x1, Pallas kernels, fused(): pl.pallas_call(functools.partial(fused_kernel, emb=EMB), out_shape=(jax.S...  107 us
    unnamed x4, local copies, waits for them, and re-layouts  2.28 us

profile of v3, /device:TPU:0, one launch (start us, length us, event | category | flops | bytes accessed | tf_op | source)
XLA Modules:
  0.0 112.2 jit_solution(16126669690839505223)
XLA Ops:
  0.6 107.4 %shard_map.67 = (f32[64,1024]{1,0:T(8,128)}, f32[1,2048]{1,0:T(1,128)}, f32[1,1]{1,0:T(1,128)}) custom-call(bf16[64,2048]{1,0:T(8,128)(2,1)} %feats.1, bf16[64,2048]{1,0:T(8,128)(2,1)} %jitter.1, s32[2,64]{1,0:T(2,128)} %bitcast.4, bf16[128,2048]{1,0:T(8,128)(2,1)} %weight.1), custom_call_target="tpu_custom_call" | custom-call | tf_op jit(solution)/shard_map/pallas_call | solution.py:447
  108.1 0.0 copy-start
  108.1 1.7 %copy.10 = f32[64,1024]{1,0:T(8,128)} copy(f32[64,1024]{1,0:T(8,128)} %get-tuple-element.12) | data formatting | bytes 524288
  109.8 0.0 copy-done
  109.8 0.6 copy.11
Async XLA Ops:
  108.1 1.7 %copy-start = (f32[1,2048]{1,0:T(1,128)S(1)}, f32[1,2048]{1,0:T(1,128)}, u32[]{:S(2)}) copy-start(f32[1,2048]{1,0:T(1,128)} %get-tuple-element.7) | copy-start | bytes 24580

commit v4 on v3

--- a/solution.py
+++ b/solution.py
@@ -198,9 +198,6 @@
         pl.when((source <= z) & (z < ZS - 1))(lambda: act(hop(v, source, 1)))
         pl.when((source >= z) & (z > 0))(lambda: act(hop(v, source, 0)))
 
-    for v in range(2):
-        hop_on(v, z, lambda copy: copy.start())
-    m_z = {d: push(ids.at[own], ids.at[own], at_z[d]) for d in (1, 2, 3)}
     second = []
 
     def forward_weight(entry):
@@ -212,7 +209,6 @@
         piece = wbuf.at[zz * QS + q_y, pl.ds(depth // 2, depth // 2)]
         second.append(push(piece, piece, beside_x))
 
-    steps = [(v, k) for v in range(2) for k in range(ZS)]
     v_s, raw_copies, crossed, stat_copies = {}, {}, {0: [], 1: []}, {}
     many = ZS * rows
 
@@ -223,22 +219,22 @@
             piece = views.at[v, block(sources[k]), mine]
             v_s[v, k] = push(piece, piece, sibling)
 
-    def project(v, k):
-        if k:
+    def project(v):
+        for k in range(1, ZS):
             v_s[v, k].wait_recv()
-        there = block(sources[k])
         flat = wbuf[...].reshape(width, cols)
-        raw[v, q, there] = jnp.dot(views[v, there], flat, preferred_element_type=F32).astype(BF)
-        piece = raw.at[v, q, there]
-        raw_copies[v, k] = push(piece, piece, beside_x), push(piece, piece, beside_y)
+        raw[v, q] = jnp.dot(views[v], flat, preferred_element_type=F32).astype(BF)
+        for k in range(2):
+            piece = raw.at[v, q, pl.ds(k * many // 2, many // 2)]
+            raw_copies[v, k] = push(piece, piece, beside_x), push(piece, piece, beside_y)
 
     def forward_raw(v, k):
-        start = pl.multiple_of(sources[k] * rows, rows)
+        start = k * many // 2
         raw_copies[v, k][0].wait_recv()
-        piece = raw.at[v, q_x, pl.ds(start, rows // 2)]
+        piece = raw.at[v, q_x, pl.ds(start, many // 4)]
         crossed[v].append(push(piece, piece, beside_y))
         raw_copies[v, k][1].wait_recv()
-        piece = raw.at[v, q_y, pl.ds(pl.multiple_of(start + rows // 2, rows // 2), rows // 2)]
+        piece = raw.at[v, q_y, pl.ds(start + many // 4, many // 4)]
         crossed[v].append(push(piece, piece, beside_x))
 
     def moments(v):
@@ -250,31 +246,31 @@
         piece = stat.at[v, q]
         stat_copies[v] = [push(piece, piece, peer) for peer in (across, beside_x, beside_y)]
 
-    w_z[1].wait_recv()
-    first.append(spread_weight(from_z[1]))
-    forward_weight(first[0])
-    for d in (3, 2):
+    for d in (1, 3, 2):
         w_z[d].wait_recv()
         first.append(spread_weight(from_z[d]))
+        if d == 1:
+            forward_weight(first[0])
+    hop_on(0, z, lambda copy: copy.start())
+    forward_weight(first[1])
     share_view(0, 1)
-    forward_weight(first[1])
+    hop_on(1, z, lambda copy: copy.start())
+    forward_weight(first[2])
     share_view(0, 2)
-    forward_weight(first[2])
+    forward_weight(first[3])
     share_view(0, 3)
-    forward_weight(first[3])
     share_view(1, 1)
     for copy in second:
         copy.wait_recv()
-    for i, step in enumerate(steps):
-        project(*step)
-        if step == (0, 1):
-            share_view(1, 2)
-        if step == (0, 3):
-            share_view(1, 3)
-        if step[1] == ZS - 1:
-            moments(step[0])
-        if i:
-            forward_raw(*steps[i - 1])
+    project(0)
+    moments(0)
+    share_view(1, 2)
+    forward_raw(0, 0)
+    share_view(1, 3)
+    forward_raw(0, 1)
+    m_z = {d: push(ids.at[own], ids.at[own], at_z[d]) for d in (1, 2, 3)}
+    project(1)
+    moments(1)
 
     inverse = {}
 
@@ -357,8 +353,9 @@
         return (inverse[v] * (grad - mean[0:1] - here * mean[1:2])).astype(BF)
 
     sib_a = gram_part(0)
-    forward_raw(*steps[-1])
+    forward_raw(1, 0)
     z_a = gram_scatter(0, sib_a)
+    forward_raw(1, 1)
     sib_b = gram_part(1)
     along_a, within_a = gram_sum(0, z_a)
     z_b = gram_scatter(1, sib_b)

time: 112 us -> 107 us (0.955)
  Pallas kernels: 107 us -> 102 us
    pallas_call x1, Pallas kernels: 107 us -> 102 us  [fused(): pl.pallas_call(functools.partial(fused_kernel, emb=EMB), out_shape=(jax.S...]
where the time goes in v4:
time: 107 us
  Pallas kernels  102 us (95%)
  between operations  2.46 us (2%)
  local copies, waits for them, and re-layouts  2.28 us (2%)
    pallas_call x1, Pallas kernels, fused(): pl.pallas_call(functools.partial(fused_kernel, emb=EMB), out_shape=(jax.S...  102 us
    unnamed x4, local copies, waits for them, and re-layouts  2.28 us

profile of v4, /device:TPU:0, one launch (start us, length us, event | category | flops | bytes accessed | tf_op | source)
XLA Modules:
  0.0 106.5 jit_solution(16582531107847179570)
XLA Ops:
  0.6 101.8 %shard_map.67 = (f32[64,1024]{1,0:T(8,128)}, f32[1,2048]{1,0:T(1,128)}, f32[1,1]{1,0:T(1,128)}) custom-call(bf16[64,2048]{1,0:T(8,128)(2,1)} %feats.1, bf16[64,2048]{1,0:T(8,128)(2,1)} %jitter.1, s32[2,64]{1,0:T(2,128)} %bitcast.4, bf16[128,2048]{1,0:T(8,128)(2,1)} %weight.1), custom_call_target="tpu_custom_call" | custom-call | tf_op jit(solution)/shard_map/pallas_call | solution.py:444
  102.4 0.0 copy-start
  102.4 1.7 %copy.10 = f32[64,1024]{1,0:T(8,128)} copy(f32[64,1024]{1,0:T(8,128)} %get-tuple-element.12) | data formatting | bytes 524288
  104.1 0.0 copy-done
  104.1 0.6 copy.11
Async XLA Ops:
  102.4 1.7 %copy-start = (f32[1,2048]{1,0:T(1,128)S(1)}, f32[1,2048]{1,0:T(1,128)}, u32[]{:S(2)}) copy-start(f32[1,2048]{1,0:T(1,128)} %get-tuple-element.7) | copy-start | bytes 24580

commit v5 on v4

--- a/solution.py
+++ b/solution.py
@@ -156,6 +156,19 @@
     own = block(z)
     mine = pl.ds(pl.multiple_of(t * half, 128), half)
 
+    def columns(d):
+        return pl.ds(pl.multiple_of(other_z[d] * cols, 128), cols)
+
+    wbuf[dp] = weight[:, columns(0)]
+    pl.semaphore_wait(barrier, len(peers))
+    w_z = {d: push(weight.at[:, columns(d)], wbuf.at[dp], at_z[d]) for d in (2, 1, 3)}
+
+    def spread_weight(zz):
+        piece = wbuf.at[zz * QS + q]
+        return push(piece, piece, beside_x), push(piece, piece, beside_y), zz
+
+    first = [spread_weight(z)]
+
     square = [lax.broadcasted_iota(jnp.int32, (rows, rows), axis) for axis in range(2)]
 
     def id_column(v):
@@ -171,18 +184,6 @@
     lanes = lax.broadcasted_iota(jnp.int32, (rows, 128), 1)
     ids[own] = jnp.where(lanes < 64, id_a, id_b)
 
-    def columns(d):
-        return pl.ds(pl.multiple_of(other_z[d] * cols, 128), cols)
-
-    wbuf[dp] = weight[:, columns(0)]
-    pl.semaphore_wait(barrier, len(peers))
-    w_z = {d: push(weight.at[:, columns(d)], wbuf.at[dp], at_z[d]) for d in (2, 1, 3)}
-
-    def spread_weight(zz):
-        piece = wbuf.at[zz * QS + q]
-        return push(piece, piece, beside_x), push(piece, piece, beside_y), zz
-
-    first = [spread_weight(z)]
 
     sources = [z, z + 1 - 2 * lax.rem(z, 2), 2 - z // 2, (ZS - 1) * (1 - z // 2)]
 
@@ -388,7 +389,7 @@
 
     order = [(1 - t, 0), (1 - t, 1), (t, 0), (t, 1)]
     gram_share(1, along_b, within_b)
-    for i, (core, c) in enumerate(order):
+    for i, (core, c) in enumerate(order[:2]):
         fown[i] = back(dz_b, core, c, 64)
     for copy in within_b:
         copy.wait_recv()
@@ -400,6 +401,8 @@
         diag_out[0:1, i * cols : (i + 1) * cols] = small[i, 0:1]
     diag_out[0:1, 0:cols] = small[0, 0:1]
     grad, copies = grad_of(0, 1, [power])
+    for i, (core, c) in enumerate(order[2:]):
+        fown[2 + i] = back(dz_b, core, c, 64)
     total = summed(1, copies)
     last[0] = total
     last_copy = push(last.at[0], last.at[1], sibling)

time: 107 us -> 106 us (level)
  no operation moved by 1% of the time
where the time goes in v5:
time: 106 us
  Pallas kernels  102 us (96%)
  between operations  2.46 us (2%)
  local copies, waits for them, and re-layouts  2.28 us (2%)
    pallas_call x1, Pallas kernels, fused(): pl.pallas_call(functools.partial(fused_kernel, emb=EMB), out_shape=(jax.S...  102 us
    unnamed x4, local copies, waits for them, and re-layouts  2.28 us

profile of v5, /device:TPU:0, one launch (start us, length us, event | category | flops | bytes accessed | tf_op | source)
XLA Modules:
  0.0 106.3 jit_solution(16043206776799369073)
XLA Ops:
  0.6 101.6 %shard_map.67 = (f32[64,1024]{1,0:T(8,128)}, f32[1,2048]{1,0:T(1,128)}, f32[1,1]{1,0:T(1,128)}) custom-call(bf16[64,2048]{1,0:T(8,128)(2,1)} %feats.1, bf16[64,2048]{1,0:T(8,128)(2,1)} %jitter.1, s32[2,64]{1,0:T(2,128)} %bitcast.4, bf16[128,2048]{1,0:T(8,128)(2,1)} %weight.1), custom_call_target="tpu_custom_call" | custom-call | tf_op jit(solution)/shard_map/pallas_call | solution.py:447
  102.2 0.0 copy-start
  102.2 1.7 %copy.10 = f32[64,1024]{1,0:T(8,128)} copy(f32[64,1024]{1,0:T(8,128)} %get-tuple-element.12) | data formatting | bytes 524288
  103.9 0.0 copy-done
  103.9 0.6 copy.11
Async XLA Ops:
  102.2 1.7 %copy-start = (f32[1,2048]{1,0:T(1,128)S(1)}, f32[1,2048]{1,0:T(1,128)}, u32[]{:S(2)}) copy-start(f32[1,2048]{1,0:T(1,128)} %get-tuple-element.7) | copy-start | bytes 24580
